TPU v7x, 32 devices: a whole 2x2x4 slice. The times are simulated.
32 devices in a mesh: angle: 8 (over y, x, core), frame: 4 (over z).
Axes of the slice: x: 2, y: 2, z: 4, core: 2. Of those that a mesh axis runs over, the one named last changes fastest.
Arguments:
- volume: float32 [32, 8192], P('frame', 'angle'), may hold values from -6 to 6
- measured: bfloat16 [8, 32, 12288], P(None, 'frame', 'angle'), may hold values from -6 to 6
- tiles: bfloat16 [8, 1024, 1536], replicated, may hold values from -0.0625 to 0.0625
- tile_index: int32 [8, 8], replicated, may hold values from 0 to 7, as said below
- warp_coef: bfloat16 [8, 3, 32, 8192], P(None, None, 'frame', 'angle'), may hold values from 0.099609375 to 0.59765625
- warp_offset: int32 [8, 32], P(None, 'frame'), may hold values from -2 to 0
- ray_weight: float32 [32, 12288], P('frame', 'angle'), may hold values from 0.5 to 2
- redundancy: float32 [12288], P('angle'), may hold values from 0.2 to 0.8
- conj_view: int32 [8, 2], P('angle'), may hold values from 0 to 1, as said below
- voxel_weight: float32 [32, 8192], P('frame', 'angle'), may hold values from 0.05 to 0.2
Outputs:
- volume_next: float32 [32, 8192], P('frame', 'angle')
- weighted: bfloat16 [8, 32, 12288], P(None, 'frame', 'angle')
Inputs may be any that keep to these rules, and one draw needn't show every extreme that they name: `conj_view`: each row is a permutation of 0..1, and row b + 4 is the inverse permutation of row b for b < 4. `tile_index`: every row is a permutation of 0..7.
All inputs are finite; a program needn't handle non-finite values.
Results may differ from a plain program's by a relative error of at most 0.0034.
Values may be sent and summed in bfloat16 or wider, within the bound.
A program may use at most 256 MiB of HBM per device.

v0:
```python
import functools

import jax
import jax.numpy as jnp
from jax import lax
from jax.experimental import pallas as pl
from jax.experimental.pallas import tpu as pltpu
from jax.sharding import PartitionSpec as P

VB = 2
HALO = 2
TAPS = 3
MESH = pl.DeviceIdType.MESH
F32 = jnp.float32
BF16 = jnp.bfloat16


def kernel(
    blocks,
    slabs,
    frames,
    rows,
    volume_hbm,
    measured_hbm,
    tiles_hbm,
    tile_index,
    coefs_hbm,
    offsets,
    weight_hbm,
    red_hbm,
    conj_view,
    voxel_hbm,
    next_hbm,
    weighted_hbm,
    volume,
    measured,
    coefs,
    ray_weight,
    redundancy,
    voxel_weight,
    next_ref,
    weighted_ref,
    tiles,
    gathered,
    proj,
    part_measured,
    part_weight,
    part_red,
    part_weighted,
    vol_out,
    vol_in,
    adj_out,
    adj_in,
    sib_out,
    sib_in,
    far_out,
    far_in,
    in_sem,
    out_sem,
    tile_sem,
    ag_send,
    ag_recv,
    fw_send,
    fw_recv,
    pt_send,
    pt_recv,
    hv_send,
    hv_recv,
    ha_send,
    ha_recv,
    sb_send,
    sb_recv,
    fr_send,
    fr_recv,
):
    me = lax.axis_index("angle")
    slab = lax.axis_index("frame")
    half = blocks // 2
    chips = blocks // 2
    core = lax.rem(me, 2)
    chip = me // 2
    sibling = me + 1 - 2 * core
    partner = lax.rem(me + half, blocks)
    count = tiles.shape[0]
    stacked = frames * rows
    sector = volume.shape[1]
    rays = measured.shape[1]
    view = rays // VB
    has_low = slab > 0
    has_high = slab < slabs - 1

    def remote(src, dst, send, recv, angle, frame=slab):
        return pltpu.make_async_remote_copy(
            src_ref=src,
            dst_ref=dst,
            send_sem=send,
            recv_sem=recv,
            device_id=(angle, frame),
            device_id_type=MESH,
        )

    def tile_copy(t):
        return pltpu.make_async_copy(tiles_hbm.at[t], tiles.at[t], tile_sem.at[t])

    barrier = pltpu.get_barrier_semaphore()
    pl.semaphore_signal(barrier, inc=1, device_id=(sibling, slab), device_id_type=MESH)
    for d in range(1, chips):
        other = lax.rem(chip + d, chips) * 2 + core
        pl.semaphore_signal(barrier, inc=1, device_id=(other, slab), device_id_type=MESH)

    @pl.when(has_low)
    def _():
        pl.semaphore_signal(barrier, inc=1, device_id=(me, slab - 1), device_id_type=MESH)

    @pl.when(has_high)
    def _():
        pl.semaphore_signal(barrier, inc=1, device_id=(me, slab + 1), device_id_type=MESH)

    local = [
        pltpu.make_async_copy(src, dst, in_sem.at[n])
        for n, (src, dst) in enumerate(
            (
                (volume_hbm, volume),
                (coefs_hbm, coefs),
                (measured_hbm, measured),
                (weight_hbm, ray_weight),
                (red_hbm, redundancy),
                (voxel_hbm, voxel_weight),
            )
        )
    ]
    for copy in local:
        copy.start()
    local[0].wait()
    vol = volume[...]
    vol_out[0] = vol[:HALO]
    vol_out[1] = vol[rows - HALO :]

    peers = chips + has_low.astype(jnp.int32) + has_high.astype(jnp.int32)
    pl.semaphore_wait(barrier, peers)

    def halo(out, into, send, recv, side):
        return remote(
            out.at[side], into.at[1 - side], send.at[side], recv.at[1 - side], me, slab + 2 * side - 1
        )

    def exchange(out, into, send, recv):
        @pl.when(has_low)
        def _():
            halo(out, into, send, recv, 0).start()

        @pl.when(has_high)
        def _():
            halo(out, into, send, recv, 1).start()

    def exchange_wait(out, into, send, recv):
        @pl.when(has_low)
        def _():
            halo(out, into, send, recv, 0).wait_send()
            halo(out, into, send, recv, 1).wait_recv()

        @pl.when(has_high)
        def _():
            halo(out, into, send, recv, 1).wait_send()
            halo(out, into, send, recv, 0).wait_recv()

        @pl.when(slab == 0)
        def _():
            into[0] = jnp.zeros_like(into[0])

        @pl.when(slab == slabs - 1)
        def _():
            into[1] = jnp.zeros_like(into[1])

    exchange(vol_out, vol_in, hv_send, hv_recv)

    off = offsets[...].astype(F32)
    lane = lax.broadcasted_iota(jnp.int32, (rows, rows), 1)
    diagonal = lane == lax.broadcasted_iota(jnp.int32, (rows, rows), 0)

    def offset_column(f):
        spread = jnp.broadcast_to(off[f : f + 1, :], (rows, rows))
        return jnp.sum(jnp.where(diagonal, spread, 0.0), axis=1, keepdims=True)

    columns = [offset_column(f) for f in range(frames)]
    group = 2 * TAPS * rows

    def warp(below, above):
        extended = jnp.concatenate([below, vol, above], axis=0)
        sources = [extended[m : m + rows] for m in range(2 * HALO + 1)]
        warped = []
        for p in range(frames // 2):
            taps = coefs[p * group : (p + 1) * group, :].astype(F32)
            for i in range(2):
                column = columns[2 * p + i]
                low = column == -2.0
                mid = column == -1.0
                total = None
                for k in range(TAPS):
                    start = (i * TAPS + k) * rows
                    chosen = jnp.where(
                        low, sources[k], jnp.where(mid, sources[k + 1], sources[k + 2])
                    )
                    term = taps[start : start + rows] * chosen
                    total = term if total is None else total + term
                warped.append(total)
        return warped

    def source(d):
        return lax.rem(chip + chips - d, chips) * 2 + core

    def cross(d, j):
        return remote(
            gathered.at[me, j],
            gathered.at[me, j],
            ag_send.at[d, j],
            ag_recv.at[d, j],
            lax.rem(chip + d, chips) * 2 + core,
        )

    def to_sibling(d, j):
        block = source(d)
        return remote(
            gathered.at[block, j],
            gathered.at[block, j],
            fw_send.at[d, j],
            fw_recv.at[d, j],
            sibling,
        )

    order = range(1, chips)

    def spread_chunk(j):
        for d in order:
            cross(d, j).start()
        to_sibling(0, j).start()

    def pass_chunk(j):
        for d in order:
            cross(d, j).wait_recv()
            to_sibling(d, j).start()

    partner_copies = [
        remote(measured_hbm, part_measured, pt_send.at[0], pt_recv.at[0], partner),
        remote(weight_hbm, part_weight, pt_send.at[1], pt_recv.at[1], partner),
        remote(red_hbm, part_red, pt_send.at[2], pt_recv.at[2], partner),
    ]
    local[1].wait()
    for t in range(count):
        tile_copy(t).start()
    outside = jnp.zeros((HALO, sector), F32)
    inner = [value[HALO : rows - HALO] for value in warp(outside, outside)]
    gathered[me, 0] = jnp.concatenate(inner, axis=0).astype(BF16)
    spread_chunk(0)
    exchange_wait(vol_out, vol_in, hv_send, hv_recv)
    outer = []
    for value in warp(vol_in[0], vol_in[1]):
        outer += [value[:HALO], value[rows - HALO :]]
    gathered[me, 1] = jnp.concatenate(outer, axis=0).astype(BF16)
    spread_chunk(1)
    for copy in partner_copies:
        copy.start()
    pass_chunk(0)
    pass_chunk(1)
    for j in range(2):
        for d in range(chips):
            to_sibling(d, j).wait_recv()

    def project(t, carry):
        tile_copy(t).wait()
        own_sector = jnp.int32(0)
        part_sector = jnp.int32(0)
        for s in range(blocks):
            own_sector = jnp.where(tile_index[me, s] == t, s, own_sector)
            part_sector = jnp.where(tile_index[partner, s] == t, s, part_sector)
        left = jnp.concatenate(
            [
                gathered[own_sector].reshape(stacked, sector),
                gathered[part_sector].reshape(stacked, sector),
            ],
            axis=0,
        )
        for n in range(VB):
            span = slice(n * view, (n + 1) * view)
            proj[:, span] += jnp.dot(left, tiles[t, :, span], preferred_element_type=F32)
        return carry

    proj[...] = jnp.zeros_like(proj)
    lax.fori_loop(0, count, project, 0)

    for copy in local[2:]:
        copy.wait()
    for copy in partner_copies:
        copy.wait_recv()

    inside = rows - 2 * HALO
    chunk = frames * inside

    def in_order(base):
        pieces = []
        for f in range(frames):
            a = base + f * inside
            b = base + chunk + f * 2 * HALO
            pieces += [proj[b : b + HALO, :], proj[a : a + inside, :], proj[b + HALO : b + 2 * HALO, :]]
        return jnp.concatenate(pieces, axis=0)

    wide = 256
    flip = lax.broadcasted_iota(jnp.int32, (wide, wide), 0) + lax.broadcasted_iota(
        jnp.int32, (wide, wide), 1
    )
    flip = jnp.where(flip == wide - 1, 1.0, 0.0).astype(BF16)
    swap = conj_view[0, 0] == 1
    residuals = [
        measured[...].astype(F32) - in_order(0),
        part_measured[...].astype(F32) - in_order(stacked),
    ]
    mirrors = []
    for value in residuals:
        high = value.astype(BF16)
        rest = (value - high.astype(F32)).astype(BF16)
        pieces = []
        for w in range(VB):
            for u in range(view // wide):
                start = w * view + view - (u + 1) * wide
                pieces.append(
                    jnp.dot(high[:, start : start + wide], flip, preferred_element_type=F32)
                    + jnp.dot(rest[:, start : start + wide], flip, preferred_element_type=F32)
                )
        each = view // wide
        head = jnp.concatenate(pieces[:each], axis=1)
        tail = jnp.concatenate(pieces[each:], axis=1)
        mirrors.append(
            jnp.concatenate(
                [jnp.where(swap, tail, head), jnp.where(swap, head, tail)], axis=1
            )
        )

    def combine(residual, mirrored, red, weight):
        red = jnp.broadcast_to(red[None, :], residual.shape)
        value = red * residual + (1.0 - red) * mirrored
        return (value * jnp.concatenate([weight] * frames, axis=0)).astype(BF16)

    weighted_ref[...] = combine(residuals[0], mirrors[1], redundancy[...], ray_weight[...])
    out_weighted = pltpu.make_async_copy(weighted_ref, weighted_hbm, out_sem.at[0])
    out_weighted.start()
    part_weighted[...] = combine(residuals[1], mirrors[0], part_red[...], part_weight[...])

    def partial(s):
        contract = (((1,), (1,)), ((), ()))
        own = lax.dot_general(
            weighted_ref[...], tiles[tile_index[me, s]], contract, preferred_element_type=F32
        )
        other = lax.dot_general(
            part_weighted[...], tiles[tile_index[partner, s]], contract, preferred_element_type=F32
        )
        return own + other

    ring = half // 2
    side = me // half
    place = lax.rem(me, half) // 2

    def sector_at(d, c):
        return side * half + lax.rem(place + d, ring) * 2 + c

    def sib_copy(d):
        return remote(sib_out.at[d], sib_in.at[d], sb_send.at[d], sb_recv.at[d], sibling)

    def far_copy(d):
        return remote(far_out.at[d], far_in.at[d], fr_send.at[d], fr_recv.at[d], sector_at(d, core))

    for d in range(1, ring):
        sib_out[d] = partial(sector_at(d, 1 - core)).astype(BF16)
        sib_copy(d).start()
    for d in range(1, ring):
        value = partial(sector_at(d, core))
        sib_copy(d).wait_recv()
        far_out[d] = (value + sib_in[d].astype(F32)).astype(BF16)
        far_copy(d).start()
    sib_out[0] = partial(sector_at(0, 1 - core)).astype(BF16)
    sib_copy(0).start()
    image = partial(me)
    for d in range(1, ring):
        far_copy(d).wait_recv()
        image = image + far_in[d].astype(F32)
    sib_copy(0).wait_recv()
    image = image + sib_in[0].astype(F32)

    spread = [jnp.zeros((rows, sector), F32) for _ in range(2 * HALO + 1)]
    for p in range(frames // 2):
        taps = coefs[p * group : (p + 1) * group, :].astype(F32)
        for i in range(2):
            f = 2 * p + i
            column = columns[f]
            slices = image[f * rows : (f + 1) * rows]
            for k in range(TAPS):
                start = (i * TAPS + k) * rows
                term = taps[start : start + rows] * slices
                for j in range(HALO + 1):
                    spread[k + j] = spread[k + j] + jnp.where(
                        column == float(j - HALO), term, 0.0
                    )
    empty = jnp.zeros((HALO, sector), F32)
    total = None
    for m in range(2 * HALO + 1):
        parts = [jnp.zeros((m, sector), F32)] if m else []
        parts.append(spread[m])
        if m < 2 * HALO:
            parts.append(jnp.zeros((2 * HALO - m, sector), F32))
        padded = jnp.concatenate(parts, axis=0)
        total = padded if total is None else total + padded
    adj_out[0] = total[:HALO]
    adj_out[1] = total[rows + HALO :]
    exchange(adj_out, adj_in, ha_send, ha_recv)
    for j in range(2):
        for d in order:
            cross(d, j).wait_send()
        for d in range(chips):
            to_sibling(d, j).wait_send()
    out_weighted.wait()
    for copy in partner_copies:
        copy.wait_send()
    for d in range(ring):
        sib_copy(d).wait_send()
    for d in range(1, ring):
        far_copy(d).wait_send()
    exchange_wait(adj_out, adj_in, ha_send, ha_recv)
    middle = jnp.zeros((rows - 2 * HALO, sector), F32)
    edges = jnp.concatenate([adj_in[0], middle, adj_in[1]], axis=0)
    adjoint = total[HALO : rows + HALO] + edges
    next_ref[...] = vol + voxel_weight[...] * adjoint
    out_next = pltpu.make_async_copy(next_ref, next_hbm, out_sem.at[1])
    out_next.start()
    out_next.wait()


def settle(next_in, weighted_in, next_out, weighted_out):
    next_out[...] = next_in[...]
    weighted_out[...] = weighted_in[...]


def body(
    volume,
    measured,
    tiles,
    tile_index,
    warp_coef,
    warp_offset,
    ray_weight,
    redundancy,
    conj_view,
    voxel_weight,
):
    frames, rows, rays = measured.shape
    sector = volume.shape[1]
    blocks = lax.axis_size("angle")
    slabs = lax.axis_size("frame")
    stacked = frames * rows
    ring = blocks // 4
    vmem = pl.BlockSpec(memory_space=pltpu.VMEM)
    hbm = pl.BlockSpec(memory_space=pl.ANY)
    smem = pl.BlockSpec(memory_space=pltpu.SMEM)
    dma = pltpu.SemaphoreType.DMA
    flops = 8 * stacked * blocks * sector * rays
    volume_next, weighted = pl.pallas_call(
        functools.partial(kernel, blocks, slabs, frames, rows),
        out_shape=(
            jax.ShapeDtypeStruct(volume.shape, F32),
            jax.ShapeDtypeStruct((stacked, rays), BF16),
        ),
        in_specs=[hbm, hbm, hbm, smem, hbm, vmem, hbm, hbm, smem, hbm],
        out_specs=(hbm, hbm),
        scratch_shapes=[
            pltpu.VMEM(volume.shape, F32),
            pltpu.VMEM((stacked, rays), BF16),
            pltpu.VMEM((frames * TAPS * rows, sector), BF16),
            pltpu.VMEM(ray_weight.shape, F32),
            pltpu.VMEM((rays,), F32),
            pltpu.VMEM(voxel_weight.shape, F32),
            pltpu.VMEM(volume.shape, F32),
            pltpu.VMEM((stacked, rays), BF16),
            pltpu.VMEM(tiles.shape, BF16),
            pltpu.VMEM((blocks, 2, stacked // 2, sector), BF16),
            pltpu.VMEM((2 * stacked, rays), F32),
            pltpu.VMEM((stacked, rays), BF16),
            pltpu.VMEM(ray_weight.shape, F32),
            pltpu.VMEM((rays,), F32),
            pltpu.VMEM((stacked, rays), BF16),
            pltpu.VMEM((2, HALO, sector), F32),
            pltpu.VMEM((2, HALO, sector), F32),
            pltpu.VMEM((2, HALO, sector), F32),
            pltpu.VMEM((2, HALO, sector), F32),
            pltpu.VMEM((ring, stacked, sector), BF16),
            pltpu.VMEM((ring, stacked, sector), BF16),
            pltpu.VMEM((ring, stacked, sector), BF16),
            pltpu.VMEM((ring, stacked, sector), BF16),
            dma((6,)),
            dma((2,)),
            dma((tiles.shape[0],)),
            dma((blocks // 2, 2)),
            dma((blocks // 2, 2)),
            dma((blocks // 2, 2)),
            dma((blocks // 2, 2)),
            dma((3,)),
            dma((3,)),
            dma((2,)),
            dma((2,)),
            dma((2,)),
            dma((2,)),
            dma((ring,)),
            dma((ring,)),
            dma((ring,)),
            dma((ring,)),
        ],
        cost_estimate=pl.CostEstimate(
            flops=flops, bytes_accessed=2 * tiles.size, transcendentals=0
        ),
        compiler_params=pltpu.CompilerParams(
            collective_id=0, has_side_effects=True, vmem_limit_bytes=62 * 1024 * 1024
        ),
    )(
        volume,
        measured.reshape(stacked, rays),
        tiles,
        tile_index,
        warp_coef.reshape(frames * TAPS * rows, sector),
        warp_offset,
        ray_weight,
        redundancy,
        conj_view,
        voxel_weight,
    )
    volume_next, weighted = pl.pallas_call(
        settle,
        out_shape=(
            jax.ShapeDtypeStruct(volume.shape, F32),
            jax.ShapeDtypeStruct((stacked, rays), BF16),
        ),
        in_specs=[vmem, vmem],
        out_specs=(vmem, vmem),
    )(volume_next, weighted)
    return volume_next, weighted.reshape(frames, rows, rays)


def solution(mesh):
    placed = (
        P("frame", "angle"),
        P(None, "frame", "angle"),
        P(),
        P(),
        P(None, None, "frame", "angle"),
        P(None, "frame"),
        P("frame", "angle"),
        P("angle"),
        P("angle", None),
        P("frame", "angle"),
    )
    return jax.shard_map(
        body,
        mesh=mesh,
        in_specs=placed,
        out_specs=(P("frame", "angle"), P(None, "frame", "angle")),
        check_vma=False,
    )
```

profile of v0, /device:TPU:0, one launch (start us, length us, event | category | flops | bytes accessed | tf_op | source)
XLA Modules:
  0.0 34.8 jit_solution(7501685225452019772)
XLA Ops:
  0.6 32.5 %shard_map.113 = (f32[8,1024]{1,0:T(8,128)}, bf16[64,1536]{1,0:T(8,128)(2,1)}) custom-call(f32[8,1024]{1,0:T(8,128)} %volume_hbm.1, bf16[64,1536]{1,0:T(8,128)(2,1)} %bitcast.4, bf16[8,1024,1536]{2,1,0:T(8,128)(2,1)} %tiles_hbm.1, s32[8,8]{1,0:T(8,128)} %tile_index.1, bf16[192,1024]{1,0:T(8,128)(2,1)} %bitcast.3, s32[8,8]{1,0:T(8,128)} %offsets.1, ...), custom_call_target="tpu_custom_call" | custom-call | flops 6442450944 | bytes 25165824 | tf_op jit(solution)/shard_map/pallas_call | solution.py:464
  33.1 1.6 %shard_map.114 = (f32[8,1024]{1,0:T(8,128)}, bf16[64,1536]{1,0:T(8,128)(2,1)}) custom-call(f32[8,1024]{1,0:T(8,128)} %get-tuple-element.6.next_in, bf16[64,1536]{1,0:T(8,128)(2,1)} %get-tuple-element.7.weighted_in), custom_call_target="tpu_custom_call" | custom-call | tf_op jit(solution)/shard_map/pallas_call | solution.py:532
where the time goes:
time: 34.9 us; the launch traced here: 34.8 us
  Pallas kernels  34.1 us (98%)
  between operations  0.64 us (2%)
    pallas_call x1, Pallas kernels, body(): pl.pallas_call(functools.partial(kernel, blocks, slabs, frames, rows), ou...  32.5 us
    pallas_call x1, Pallas kernels, body(): pl.pallas_call(settle, out_shape=(jax.ShapeDtypeStruct(volume.shape, F32)...  1.64 us

commit v1 on v0

v1 whole, which is shorter than its diff:
```python
import functools

import jax
import jax.numpy as jnp
from jax import lax
from jax.experimental import pallas as pl
from jax.experimental.pallas import tpu as pltpu
from jax.sharding import PartitionSpec as P

VB = 2
HALO = 2
TAPS = 3
MESH = pl.DeviceIdType.MESH
F32 = jnp.float32
BF16 = jnp.bfloat16


def kernel(
    blocks,
    slabs,
    frames,
    rows,
    volume_hbm,
    measured_hbm,
    tiles_hbm,
    index_hbm,
    coefs_hbm,
    offsets_hbm,
    weight_hbm,
    red_hbm,
    conj_hbm,
    voxel_hbm,
    next_hbm,
    weighted_hbm,
    volume,
    measured,
    coefs,
    offsets,
    ray_weight,
    redundancy,
    voxel_weight,
    tile_index,
    conj_view,
    find,
    next_ref,
    tiles,
    gathered,
    away,
    proj_mine,
    proj_out,
    proj_in,
    part_measured,
    part_weight,
    part_red,
    wall,
    wall_in,
    product,
    image,
    vol_out,
    vol_in,
    adj_out,
    adj_in,
    sib_out,
    sib_in,
    far_out,
    far_in,
    in_sem,
    out_sem,
    tile_sem,
    ag_send,
    ag_recv,
    fw_send,
    fw_recv,
    pt_send,
    pt_recv,
    pj_send,
    pj_recv,
    wt_send,
    wt_recv,
    hv_send,
    hv_recv,
    ha_send,
    ha_recv,
    sb_send,
    sb_recv,
    fr_send,
    fr_recv,
):
    me = lax.axis_index("angle")
    slab = lax.axis_index("frame")
    chips = blocks // 2
    ring = chips // 2
    core = lax.rem(me, 2)
    chip = me // 2
    half = chip // ring
    place = lax.rem(chip, ring)
    sibling = me + 1 - 2 * core

    def chip_at(dh, dp):
        return lax.rem(half + dh, 2) * ring + lax.rem(place + dp, ring)

    def chip_from(dh, dp):
        return lax.rem(half + dh, 2) * ring + lax.rem(place + ring - dp, ring)

    partner = 2 * chip_at(1, 0) + core
    group = [me, partner, sibling, 2 * chip_at(1, 0) + 1 - core]
    others = [(dh, dp) for dp in range(ring) for dh in range(2) if dh or dp]
    everyone = [(0, 0)] + others
    count = tiles.shape[0]
    first = core * count
    stacked = frames * rows // 2
    sector = volume.shape[1]
    rays = measured.shape[1]
    view = rays // VB
    has_low = slab > 0
    has_high = slab < slabs - 1

    def remote(src, dst, send, recv, angle, frame=slab):
        return pltpu.make_async_remote_copy(
            src_ref=src,
            dst_ref=dst,
            send_sem=send,
            recv_sem=recv,
            device_id=(angle, frame),
            device_id_type=MESH,
        )

    def tile_copy(t):
        return pltpu.make_async_copy(tiles_hbm.at[first + t], tiles.at[t], tile_sem.at[t])

    barrier = pltpu.get_barrier_semaphore()
    pl.semaphore_signal(barrier, inc=1, device_id=(sibling, slab), device_id_type=MESH)
    for dh, dp in others:
        pl.semaphore_signal(
            barrier, inc=1, device_id=(2 * chip_at(dh, dp) + core, slab), device_id_type=MESH
        )

    @pl.when(has_low)
    def _():
        pl.semaphore_signal(barrier, inc=1, device_id=(me, slab - 1), device_id_type=MESH)

    @pl.when(has_high)
    def _():
        pl.semaphore_signal(barrier, inc=1, device_id=(me, slab + 1), device_id_type=MESH)

    measured_half = measured_hbm.at[pl.ds(pl.multiple_of(half * stacked, 16), stacked)]
    measured_away = measured_hbm.at[pl.ds(pl.multiple_of((1 - half) * stacked, 16), stacked)]
    local = [
        pltpu.make_async_copy(src, dst, in_sem.at[n])
        for n, (src, dst) in enumerate(
            (
                (volume_hbm, volume),
                (coefs_hbm, coefs),
                (offsets_hbm, offsets),
                (index_hbm, tile_index),
                (conj_hbm, conj_view),
                (measured_half, measured),
                (weight_hbm, ray_weight),
                (red_hbm, redundancy),
                (voxel_hbm, voxel_weight),
            )
        )
    ]
    for copy in local:
        copy.start()
    local[0].wait()
    vol = volume[...]
    vol_out[0] = vol[:HALO]
    vol_out[1] = vol[rows - HALO :]

    peers = chips + has_low.astype(jnp.int32) + has_high.astype(jnp.int32)
    pl.semaphore_wait(barrier, peers)

    def halo(out, into, send, recv, side):
        return remote(
            out.at[side], into.at[1 - side], send.at[side], recv.at[1 - side], me, slab + 2 * side - 1
        )

    def exchange(out, into, send, recv):
        @pl.when(has_low)
        def _():
            halo(out, into, send, recv, 0).start()

        @pl.when(has_high)
        def _():
            halo(out, into, send, recv, 1).start()

    def exchange_wait(out, into, send, recv):
        @pl.when(has_low)
        def _():
            halo(out, into, send, recv, 0).wait_send()
            halo(out, into, send, recv, 1).wait_recv()

        @pl.when(has_high)
        def _():
            halo(out, into, send, recv, 1).wait_send()
            halo(out, into, send, recv, 0).wait_recv()

        @pl.when(slab == 0)
        def _():
            into[0] = jnp.zeros_like(into[0])

        @pl.when(slab == slabs - 1)
        def _():
            into[1] = jnp.zeros_like(into[1])

    exchange(vol_out, vol_in, hv_send, hv_recv)
    local[1].wait()
    local[2].wait()

    off = offsets[...].astype(F32)
    lane = lax.broadcasted_iota(jnp.int32, (rows, rows), 1)
    diagonal = lane == lax.broadcasted_iota(jnp.int32, (rows, rows), 0)

    def offset_column(f):
        spread = jnp.broadcast_to(off[f : f + 1, :], (rows, rows))
        return jnp.sum(jnp.where(diagonal, spread, 0.0), axis=1, keepdims=True)

    columns = [offset_column(f) for f in range(frames)]
    pair = 2 * TAPS * rows

    def warp(below, above):
        extended = jnp.concatenate([below, vol, above], axis=0)
        sources = [extended[m : m + rows] for m in range(2 * HALO + 1)]
        warped = []
        for p in range(frames // 2):
            taps = coefs[p * pair : (p + 1) * pair, :].astype(F32)
            for i in range(2):
                column = columns[2 * p + i]
                low = column == -2.0
                mid = column == -1.0
                total = None
                for k in range(TAPS):
                    start = (i * TAPS + k) * rows
                    chosen = jnp.where(
                        low, sources[k], jnp.where(mid, sources[k + 1], sources[k + 2])
                    )
                    term = taps[start : start + rows] * chosen
                    total = term if total is None else total + term
                warped.append(total)
        return warped

    def keep(j, pieces):
        each = len(pieces) // 2
        early = jnp.concatenate(pieces[:each], axis=0)
        late = jnp.concatenate(pieces[each:], axis=0)
        gathered[me, j] = jnp.where(half == 0, early, late).astype(BF16)
        away[j] = jnp.where(half == 0, late, early).astype(BF16)

    def slot(dh, dp):
        return dh * ring + dp

    def cross(dh, dp, j):
        return remote(
            away.at[j] if dh else gathered.at[me, j],
            gathered.at[me, j],
            ag_send.at[slot(dh, dp), j],
            ag_recv.at[slot(dh, dp), j],
            2 * chip_at(dh, dp) + core,
        )

    def to_sibling(dh, dp, j):
        block = 2 * chip_from(dh, dp) + core
        return remote(
            gathered.at[block, j],
            gathered.at[block, j],
            fw_send.at[slot(dh, dp), j],
            fw_recv.at[slot(dh, dp), j],
            sibling,
        )

    def spread_chunk(j):
        for dh, dp in reversed(others):
            cross(dh, dp, j).start()
        to_sibling(0, 0, j).start()

    def pass_chunk(j):
        for dh, dp in others:
            cross(dh, dp, j).wait_recv()
            to_sibling(dh, dp, j).start()

    partner_copies = [
        remote(measured_away, part_measured, pt_send.at[0], pt_recv.at[0], partner),
        remote(weight_hbm, part_weight, pt_send.at[1], pt_recv.at[1], partner),
        remote(red_hbm, part_red, pt_send.at[2], pt_recv.at[2], partner),
    ]
    outside = jnp.zeros((HALO, sector), F32)
    keep(0, [value[HALO : rows - HALO] for value in warp(outside, outside)])
    spread_chunk(0)
    for t in range(count):
        tile_copy(t).start()
    for copy in partner_copies[1:]:
        copy.start()
    exchange_wait(vol_out, vol_in, hv_send, hv_recv)
    outer = []
    for value in warp(vol_in[0], vol_in[1]):
        outer += [jnp.concatenate([value[:HALO], value[rows - HALO :]], axis=0)]
    keep(1, outer)
    spread_chunk(1)
    partner_copies[0].start()

    local[3].wait()
    for q in range(4):
        row = [tile_index[group[q], s] for s in range(blocks)]
        for t in range(count):
            at = jnp.int32(0)
            for s in range(blocks):
                at = jnp.where(row[s] == first + t, s, at)
            find[q, t] = at

    pass_chunk(0)
    pass_chunk(1)
    for t in range(count):
        tile_copy(t).wait()
    for j in range(2):
        for dh, dp in everyone:
            to_sibling(dh, dp, j).wait_recv()

    wide = 256
    parts = rays // wide
    each = view // wide

    def proj_copy(n):
        return remote(proj_out.at[n], proj_in.at[n], pj_send.at[n], pj_recv.at[n], sibling)

    for n in range(parts):
        total = None
        for t in range(count):
            left = jnp.concatenate(
                [gathered[find[q, t]].reshape(stacked, sector) for q in range(4)], axis=0
            )
            term = jnp.dot(
                left, tiles[t, :, n * wide : (n + 1) * wide], preferred_element_type=F32
            )
            total = term if total is None else total + term
        proj_mine[n] = total[: 2 * stacked]
        proj_out[n] = total[2 * stacked :]
        proj_copy(n).start()

    for copy in local[4:]:
        copy.wait()
    for copy in partner_copies:
        copy.wait_recv()

    inside = rows - 2 * HALO
    chunk = frames * inside // 2

    def in_order(value, base):
        pieces = []
        for f in range(frames // 2):
            a = base + f * inside
            b = base + chunk + f * 2 * HALO
            pieces += [value[b : b + HALO], value[a : a + inside], value[b + HALO : b + 2 * HALO]]
        return jnp.concatenate(pieces, axis=0)

    flip = lax.broadcasted_iota(jnp.int32, (wide, wide), 0) + lax.broadcasted_iota(
        jnp.int32, (wide, wide), 1
    )
    flip = jnp.where(flip == wide - 1, 1.0, 0.0).astype(BF16)
    swap = conj_view[0, 0] == 1
    residuals = []
    flipped = []
    for n in range(parts):
        span = slice(n * wide, (n + 1) * wide)
        proj_copy(n).wait_recv()
        value = proj_mine[n] + proj_in[n]
        value = jnp.concatenate(
            [
                measured[:, span].astype(F32) - in_order(value, 0),
                part_measured[:, span].astype(F32) - in_order(value, stacked),
            ],
            axis=0,
        )
        high = value.astype(BF16)
        rest = (value - high.astype(F32)).astype(BF16)
        residuals.append(value)
        flipped.append(
            jnp.dot(high, flip, preferred_element_type=F32)
            + jnp.dot(rest, flip, preferred_element_type=F32)
        )

    def combine(residual, mirrored, red, weight):
        red = jnp.broadcast_to(red, residual.shape)
        value = red * residual + (1.0 - red) * mirrored
        return (value * jnp.concatenate([weight] * (frames // 2), axis=0)).astype(BF16)

    red_own = redundancy[...][None, :]
    red_part = part_red[...][None, :]
    for w in range(VB):
        for u in range(each):
            n = w * each + u
            span = slice(n * wide, (n + 1) * wide)
            straight = flipped[w * each + each - 1 - u]
            crossed = flipped[(VB - 1 - w) * each + each - 1 - u]
            mirrored = jnp.where(swap, crossed, straight)
            wall[:stacked, span] = combine(
                residuals[n][:stacked], mirrored[stacked:], red_own[:, span], ray_weight[:, span]
            )
            wall[stacked:, span] = combine(
                residuals[n][stacked:], mirrored[:stacked], red_part[:, span], part_weight[:, span]
            )

    wall_copy = remote(wall, wall_in, wt_send.at[0], wt_recv.at[0], sibling)
    wall_copy.start()
    place_rows = pl.ds(pl.multiple_of(half * stacked, 16), stacked)
    out_weighted = pltpu.make_async_copy(
        wall.at[pl.ds(0, stacked)], weighted_hbm.at[place_rows], out_sem.at[0]
    )
    out_weighted.start()
    back_copy = remote(
        wall.at[pl.ds(stacked, stacked)],
        weighted_hbm.at[place_rows],
        wt_send.at[1],
        wt_recv.at[1],
        partner,
    )
    back_copy.start()
    wall_copy.wait_recv()

    cuts = 2
    width = sector // cuts

    def multiply(c):
        both = jnp.concatenate([wall[...], wall_in[...]], axis=0)
        for t in range(count):
            product[c, t] = lax.dot_general(
                both,
                tiles[t, c * width : (c + 1) * width, :],
                (((1,), (1,)), ((), ())),
                preferred_element_type=F32,
            )

    def partial(c, s):
        total = None
        for q in range(4):
            t = tile_index[group[q], s] - first
            ours = jnp.logical_and(t >= 0, t < count)
            t = jnp.where(ours, t, 0)
            term = jnp.where(ours, product[c, t, q * stacked : (q + 1) * stacked, :], 0.0)
            total = term if total is None else total + term
        return total

    def sib_copy(c):
        return remote(sib_out.at[c], sib_in.at[c], sb_send.at[c], sb_recv.at[c], sibling)

    def far_copy(c, dh, dp):
        i = slot(dh, dp)
        return remote(
            far_out.at[c, i],
            far_in.at[c, i],
            fr_send.at[c, i],
            fr_recv.at[c, i],
            2 * chip_at(dh, dp) + core,
        )

    def give(c):
        for dh, dp in everyone:
            sib_out[c, slot(dh, dp)] = partial(c, 2 * chip_at(dh, dp) + 1 - core).astype(BF16)
        sib_copy(c).start()

    def pass_on(c):
        for n, (dh, dp) in enumerate(reversed(everyone)):
            i = slot(dh, dp)
            value = partial(c, 2 * chip_at(dh, dp) + core)
            if n == 0:
                sib_copy(c).wait_recv()
            value = value + sib_in[c, i].astype(F32)
            if (dh, dp) == (0, 0):
                image[half, :, c * width : (c + 1) * width] = value
            else:
                far_out[c, i] = value.astype(BF16)
                far_copy(c, dh, dp).start()

    def collect(c):
        span = slice(c * width, (c + 1) * width)
        same = image[half, :, span]
        other = None
        for dh, dp in others:
            far_copy(c, dh, dp).wait_recv()
            value = far_in[c, slot(dh, dp)].astype(F32)
            if dh:
                other = value if other is None else other + value
            else:
                same = same + value
        image[half, :, span] = same
        image[1 - half, :, span] = other

    multiply(0)
    give(0)
    for c in range(1, cuts):
        multiply(c)
        give(c)
        pass_on(c - 1)
    pass_on(cuts - 1)
    for c in range(cuts):
        collect(c)

    spread = [jnp.zeros((rows, sector), F32) for _ in range(2 * HALO + 1)]
    for p in range(frames // 2):
        taps = coefs[p * pair : (p + 1) * pair, :].astype(F32)
        for i in range(2):
            f = 2 * p + i
            column = columns[f]
            g = f % (frames // 2)
            slices = image[f // (frames // 2), g * rows : (g + 1) * rows, :]
            for k in range(TAPS):
                start = (i * TAPS + k) * rows
                term = taps[start : start + rows] * slices
                for j in range(HALO + 1):
                    spread[k + j] = spread[k + j] + jnp.where(
                        column == float(j - HALO), term, 0.0
                    )
    total = None
    for m in range(2 * HALO + 1):
        pieces = [jnp.zeros((m, sector), F32)] if m else []
        pieces.append(spread[m])
        if m < 2 * HALO:
            pieces.append(jnp.zeros((2 * HALO - m, sector), F32))
        padded = jnp.concatenate(pieces, axis=0)
        total = padded if total is None else total + padded
    adj_out[0] = total[:HALO]
    adj_out[1] = total[rows + HALO :]
    exchange(adj_out, adj_in, ha_send, ha_recv)
    for j in range(2):
        for dh, dp in others:
            cross(dh, dp, j).wait_send()
        for dh, dp in everyone:
            to_sibling(dh, dp, j).wait_send()
    for copy in partner_copies:
        copy.wait_send()
    for n in range(parts):
        proj_copy(n).wait_send()
    wall_copy.wait_send()
    back_copy.wait()
    out_weighted.wait()
    for c in range(cuts):
        sib_copy(c).wait_send()
        for dh, dp in others:
            far_copy(c, dh, dp).wait_send()
    exchange_wait(adj_out, adj_in, ha_send, ha_recv)
    middle = jnp.zeros((rows - 2 * HALO, sector), F32)
    edges = jnp.concatenate([adj_in[0], middle, adj_in[1]], axis=0)
    adjoint = total[HALO : rows + HALO] + edges
    next_ref[...] = vol + voxel_weight[...] * adjoint
    out_next = pltpu.make_async_copy(next_ref, next_hbm, out_sem.at[1])
    out_next.start()
    out_next.wait()


def settle(next_in, weighted_in, next_out, weighted_out):
    next_out[...] = next_in[...]
    weighted_out[...] = weighted_in[...]


def body(
    volume,
    measured,
    tiles,
    tile_index,
    warp_coef,
    warp_offset,
    ray_weight,
    redundancy,
    conj_view,
    voxel_weight,
):
    frames, rows, rays = measured.shape
    sector = volume.shape[1]
    blocks = lax.axis_size("angle")
    slabs = lax.axis_size("frame")
    stacked = frames * rows
    chips = blocks // 2
    mine = tiles.shape[0] // 2
    parts = rays // 256
    cuts = 2
    vmem = pl.BlockSpec(memory_space=pltpu.VMEM)
    hbm = pl.BlockSpec(memory_space=pl.ANY)
    dma = pltpu.SemaphoreType.DMA
    flops = 4 * stacked * blocks * sector * rays
    volume_next, weighted = pl.pallas_call(
        functools.partial(kernel, blocks, slabs, frames, rows),
        out_shape=(
            jax.ShapeDtypeStruct(volume.shape, F32),
            jax.ShapeDtypeStruct((stacked, rays), BF16),
        ),
        in_specs=[hbm] * 10,
        out_specs=(hbm, hbm),
        scratch_shapes=[
            pltpu.VMEM(volume.shape, F32),
            pltpu.VMEM((stacked // 2, rays), BF16),
            pltpu.VMEM((frames * TAPS * rows, sector), BF16),
            pltpu.VMEM(warp_offset.shape, jnp.int32),
            pltpu.VMEM(ray_weight.shape, F32),
            pltpu.VMEM((rays,), F32),
            pltpu.VMEM(voxel_weight.shape, F32),
            pltpu.SMEM(tile_index.shape, jnp.int32),
            pltpu.SMEM(conj_view.shape, jnp.int32),
            pltpu.SMEM((4, mine), jnp.int32),
            pltpu.VMEM(volume.shape, F32),
            pltpu.VMEM((mine,) + tiles.shape[1:], BF16),
            pltpu.VMEM((blocks, 2, stacked // 4, sector), BF16),
            pltpu.VMEM((2, stacked // 4, sector), BF16),
            pltpu.VMEM((parts, stacked, 256), F32),
            pltpu.VMEM((parts, stacked, 256), F32),
            pltpu.VMEM((parts, stacked, 256), F32),
            pltpu.VMEM((stacked // 2, rays), BF16),
            pltpu.VMEM(ray_weight.shape, F32),
            pltpu.VMEM((rays,), F32),
            pltpu.VMEM((stacked, rays), BF16),
            pltpu.VMEM((stacked, rays), BF16),
            pltpu.VMEM((cuts, mine, 2 * stacked, sector // cuts), F32),
            pltpu.VMEM((2, stacked // 2, sector), F32),
            pltpu.VMEM((2, HALO, sector), F32),
            pltpu.VMEM((2, HALO, sector), F32),
            pltpu.VMEM((2, HALO, sector), F32),
            pltpu.VMEM((2, HALO, sector), F32),
            pltpu.VMEM((cuts, chips, stacked // 2, sector // cuts), BF16),
            pltpu.VMEM((cuts, chips, stacked // 2, sector // cuts), BF16),
            pltpu.VMEM((cuts, chips, stacked // 2, sector // cuts), BF16),
            pltpu.VMEM((cuts, chips, stacked // 2, sector // cuts), BF16),
            dma((9,)),
            dma((2,)),
            dma((mine,)),
            dma((chips, 2)),
            dma((chips, 2)),
            dma((chips, 2)),
            dma((chips, 2)),
            dma((3,)),
            dma((3,)),
            dma((parts,)),
            dma((parts,)),
            dma((2,)),
            dma((2,)),
            dma((2,)),
            dma((2,)),
            dma((2,)),
            dma((2,)),
            dma((cuts,)),
            dma((cuts,)),
            dma((cuts, chips)),
            dma((cuts, chips)),
        ],
        cost_estimate=pl.CostEstimate(
            flops=flops, bytes_accessed=2 * tiles.size, transcendentals=0
        ),
        compiler_params=pltpu.CompilerParams(
            collective_id=0, has_side_effects=True, vmem_limit_bytes=62 * 1024 * 1024
        ),
    )(
        volume,
        measured.reshape(stacked, rays),
        tiles,
        tile_index,
        warp_coef.reshape(frames * TAPS * rows, sector),
        warp_offset,
        ray_weight,
        redundancy,
        conj_view,
        voxel_weight,
    )
    volume_next, weighted = pl.pallas_call(
        settle,
        out_shape=(
            jax.ShapeDtypeStruct(volume.shape, F32),
            jax.ShapeDtypeStruct((stacked, rays), BF16),
        ),
        in_specs=[vmem, vmem],
        out_specs=(vmem, vmem),
    )(volume_next, weighted)
    return volume_next, weighted.reshape(frames, rows, rays)


def solution(mesh):
    placed = (
        P("frame", "angle"),
        P(None, "frame", "angle"),
        P(),
        P(),
        P(None, None, "frame", "angle"),
        P(None, "frame"),
        P("frame", "angle"),
        P("angle"),
        P("angle", None),
        P("frame", "angle"),
    )
    return jax.shard_map(
        body,
        mesh=mesh,
        in_specs=placed,
        out_specs=(P("frame", "angle"), P(None, "frame", "angle")),
        check_vma=False,
    )
```

time: 34.9 us -> 35.1 us (level)
  no operation moved by 1% of the time
where the time goes in v1:
time: 35.1 us; the launch traced here: 35 us
  Pallas kernels  34.3 us (98%)
  between operations  0.64 us (2%)
    pallas_call x1, Pallas kernels, body(): pl.pallas_call(functools.partial(kernel, blocks, slabs, frames, rows), ou...  32.7 us
    pallas_call x1, Pallas kernels, body(): pl.pallas_call(settle, out_shape=(jax.ShapeDtypeStruct(volume.shape, F32)...  1.64 us

profile of v1, /device:TPU:0, one launch (start us, length us, event | category | flops | bytes accessed | tf_op | source)
XLA Modules:
  0.0 35.0 jit_solution(3162689192491387727)
XLA Ops:
  0.6 32.7 %shard_map.113 = (f32[8,1024]{1,0:T(8,128)}, bf16[64,1536]{1,0:T(8,128)(2,1)}) custom-call(f32[8,1024]{1,0:T(8,128)} %volume_hbm.1, bf16[64,1536]{1,0:T(8,128)(2,1)} %bitcast.4, bf16[8,1024,1536]{2,1,0:T(8,128)(2,1)} %tiles_hbm.1, s32[8,8]{1,0:T(8,128)} %index_hbm.1, bf16[192,1024]{1,0:T(8,128)(2,1)} %bitcast.3, s32[8,8]{1,0:T(8,128)} %offsets_hbm.1, ...), custom_call_target="tpu_custom_call" | custom-call | flops 3221225472 | bytes 25165824 | tf_op jit(solution)/shard_map/pallas_call | solution.py:580
  33.3 1.6 %shard_map.114 = (f32[8,1024]{1,0:T(8,128)}, bf16[64,1536]{1,0:T(8,128)(2,1)}) custom-call(f32[8,1024]{1,0:T(8,128)} %get-tuple-element.6.next_in, bf16[64,1536]{1,0:T(8,128)(2,1)} %get-tuple-element.7.weighted_in), custom_call_target="tpu_custom_call" | custom-call | tf_op jit(solution)/shard_map/pallas_call | solution.py:661

commit v2 on v1

--- a/solution.py
+++ b/solution.py
@@ -30,7 +30,8 @@
     red_hbm,
     conj_hbm,
     voxel_hbm,
-    next_hbm,
+    base_hbm,
+    edges_hbm,
     weighted_hbm,
     volume,
     measured,
@@ -42,8 +43,10 @@
     tile_index,
     conj_view,
     find,
-    next_ref,
+    base,
+    zeros,
     tiles,
+    turned,
     gathered,
     away,
     proj_mine,
@@ -59,13 +62,13 @@
     vol_out,
     vol_in,
     adj_out,
-    adj_in,
     sib_out,
     sib_in,
     far_out,
     far_in,
     in_sem,
     out_sem,
+    zero_sem,
     tile_sem,
     ag_send,
     ag_recv,
@@ -163,6 +166,8 @@
     ]
     for copy in local:
         copy.start()
+    for t in range(count):
+        tile_copy(t).start()
     local[0].wait()
     vol = volume[...]
     vol_out[0] = vol[:HALO]
@@ -195,14 +200,6 @@
         def _():
             halo(out, into, send, recv, 1).wait_send()
             halo(out, into, send, recv, 0).wait_recv()
-
-        @pl.when(slab == 0)
-        def _():
-            into[0] = jnp.zeros_like(into[0])
-
-        @pl.when(slab == slabs - 1)
-        def _():
-            into[1] = jnp.zeros_like(into[1])
 
     exchange(vol_out, vol_in, hv_send, hv_recv)
     local[1].wait()
@@ -284,20 +281,45 @@
         remote(weight_hbm, part_weight, pt_send.at[1], pt_recv.at[1], partner),
         remote(red_hbm, part_red, pt_send.at[2], pt_recv.at[2], partner),
     ]
+    block = 128
+
+    def turn(t):
+        tile_copy(t).wait()
+
+        def step(n, carry):
+            span = pl.ds(pl.multiple_of(n * block, block), block)
+            turned[t, :, span] = tiles[t, span, :].T
+            return carry
+
+        lax.fori_loop(0, sector // block, step, 0)
+
     outside = jnp.zeros((HALO, sector), F32)
     keep(0, [value[HALO : rows - HALO] for value in warp(outside, outside)])
     spread_chunk(0)
-    for t in range(count):
-        tile_copy(t).start()
+    turn(0)
     for copy in partner_copies[1:]:
         copy.start()
     exchange_wait(vol_out, vol_in, hv_send, hv_recv)
+
+    @pl.when(slab == 0)
+    def _():
+        vol_in[0] = jnp.zeros_like(vol_in[0])
+        zeros[...] = jnp.zeros_like(zeros)
+        pltpu.make_async_copy(zeros, edges_hbm.at[0], zero_sem.at[0]).start()
+
+    @pl.when(slab == slabs - 1)
+    def _():
+        vol_in[1] = jnp.zeros_like(vol_in[1])
+        zeros[...] = jnp.zeros_like(zeros)
+        pltpu.make_async_copy(zeros, edges_hbm.at[1], zero_sem.at[0]).start()
+
     outer = []
     for value in warp(vol_in[0], vol_in[1]):
         outer += [jnp.concatenate([value[:HALO], value[rows - HALO :]], axis=0)]
     keep(1, outer)
     spread_chunk(1)
     partner_copies[0].start()
+    turn(1)
 
     local[3].wait()
     for q in range(4):
@@ -309,34 +331,32 @@
             find[q, t] = at
 
     pass_chunk(0)
+    turn(2)
     pass_chunk(1)
-    for t in range(count):
+    for t in range(turned.shape[0], count):
         tile_copy(t).wait()
     for j in range(2):
         for dh, dp in everyone:
             to_sibling(dh, dp, j).wait_recv()
 
-    wide = 256
-    parts = rays // wide
-    each = view // wide
-
-    def proj_copy(n):
-        return remote(proj_out.at[n], proj_in.at[n], pj_send.at[n], pj_recv.at[n], sibling)
-
-    for n in range(parts):
+    def proj_copy(w):
+        return remote(proj_out.at[w], proj_in.at[w], pj_send.at[w], pj_recv.at[w], sibling)
+
+    for w in range(VB):
         total = None
         for t in range(count):
             left = jnp.concatenate(
                 [gathered[find[q, t]].reshape(stacked, sector) for q in range(4)], axis=0
             )
             term = jnp.dot(
-                left, tiles[t, :, n * wide : (n + 1) * wide], preferred_element_type=F32
+                left, tiles[t, :, w * view : (w + 1) * view], preferred_element_type=F32
             )
             total = term if total is None else total + term
-        proj_mine[n] = total[: 2 * stacked]
-        proj_out[n] = total[2 * stacked :]
-        proj_copy(n).start()
-
+        proj_mine[w] = total[: 2 * stacked]
+        proj_out[w] = total[2 * stacked :]
+
+    for w in range(VB):
+        proj_copy(w).start()
     for copy in local[4:]:
         copy.wait()
     for copy in partner_copies:
@@ -353,6 +373,8 @@
             pieces += [value[b : b + HALO], value[a : a + inside], value[b + HALO : b + 2 * HALO]]
         return jnp.concatenate(pieces, axis=0)
 
+    wide = 256
+    each = view // wide
     flip = lax.broadcasted_iota(jnp.int32, (wide, wide), 0) + lax.broadcasted_iota(
         jnp.int32, (wide, wide), 1
     )
@@ -360,10 +382,10 @@
     swap = conj_view[0, 0] == 1
     residuals = []
     flipped = []
-    for n in range(parts):
-        span = slice(n * wide, (n + 1) * wide)
-        proj_copy(n).wait_recv()
-        value = proj_mine[n] + proj_in[n]
+    for w in range(VB):
+        span = slice(w * view, (w + 1) * view)
+        proj_copy(w).wait_recv()
+        value = proj_mine[w] + proj_in[w]
         value = jnp.concatenate(
             [
                 measured[:, span].astype(F32) - in_order(value, 0),
@@ -371,12 +393,19 @@
             ],
             axis=0,
         )
-        high = value.astype(BF16)
-        rest = (value - high.astype(F32)).astype(BF16)
         residuals.append(value)
+        tall = jnp.concatenate(
+            [value[:, u * wide : (u + 1) * wide] for u in reversed(range(each))], axis=0
+        )
+        high = tall.astype(BF16)
+        rest = (tall - high.astype(F32)).astype(BF16)
+        tall = jnp.dot(high, flip, preferred_element_type=F32) + jnp.dot(
+            rest, flip, preferred_element_type=F32
+        )
         flipped.append(
-            jnp.dot(high, flip, preferred_element_type=F32)
-            + jnp.dot(rest, flip, preferred_element_type=F32)
+            jnp.concatenate(
+                [tall[u * 2 * stacked : (u + 1) * 2 * stacked] for u in range(each)], axis=1
+            )
         )
 
     def combine(residual, mirrored, red, weight):
@@ -384,51 +413,64 @@
         value = red * residual + (1.0 - red) * mirrored
         return (value * jnp.concatenate([weight] * (frames // 2), axis=0)).astype(BF16)
 
+    def wall_copy(w):
+        return remote(wall.at[w], wall_in.at[w], wt_send.at[0, w], wt_recv.at[0, w], sibling)
+
+    place_rows = pl.ds(pl.multiple_of(half * stacked, 16), stacked)
+
+    def out_weighted(w):
+        return pltpu.make_async_copy(
+            wall.at[w, pl.ds(0, stacked)],
+            weighted_hbm.at[place_rows, pl.ds(w * view, view)],
+            out_sem.at[1 + w],
+        )
+
+    def back_copy(w):
+        return remote(
+            wall.at[w, pl.ds(stacked, stacked)],
+            weighted_hbm.at[place_rows, pl.ds(w * view, view)],
+            wt_send.at[1, w],
+            wt_recv.at[1, w],
+            partner,
+        )
+
     red_own = redundancy[...][None, :]
     red_part = part_red[...][None, :]
     for w in range(VB):
-        for u in range(each):
-            n = w * each + u
-            span = slice(n * wide, (n + 1) * wide)
-            straight = flipped[w * each + each - 1 - u]
-            crossed = flipped[(VB - 1 - w) * each + each - 1 - u]
-            mirrored = jnp.where(swap, crossed, straight)
-            wall[:stacked, span] = combine(
-                residuals[n][:stacked], mirrored[stacked:], red_own[:, span], ray_weight[:, span]
-            )
-            wall[stacked:, span] = combine(
-                residuals[n][stacked:], mirrored[:stacked], red_part[:, span], part_weight[:, span]
-            )
-
-    wall_copy = remote(wall, wall_in, wt_send.at[0], wt_recv.at[0], sibling)
-    wall_copy.start()
-    place_rows = pl.ds(pl.multiple_of(half * stacked, 16), stacked)
-    out_weighted = pltpu.make_async_copy(
-        wall.at[pl.ds(0, stacked)], weighted_hbm.at[place_rows], out_sem.at[0]
-    )
-    out_weighted.start()
-    back_copy = remote(
-        wall.at[pl.ds(stacked, stacked)],
-        weighted_hbm.at[place_rows],
-        wt_send.at[1],
-        wt_recv.at[1],
-        partner,
-    )
-    back_copy.start()
-    wall_copy.wait_recv()
-
-    cuts = 2
+        span = slice(w * view, (w + 1) * view)
+        mirrored = jnp.where(swap, flipped[VB - 1 - w], flipped[w])
+        wall[w, :stacked] = combine(
+            residuals[w][:stacked], mirrored[stacked:], red_own[:, span], ray_weight[:, span]
+        )
+        wall[w, stacked:] = combine(
+            residuals[w][stacked:], mirrored[:stacked], red_part[:, span], part_weight[:, span]
+        )
+        wall_copy(w).start()
+    for w in range(VB):
+        back_copy(w).start()
+        out_weighted(w).start()
+
+    cuts = product.shape[0]
     width = sector // cuts
 
-    def multiply(c):
-        both = jnp.concatenate([wall[...], wall_in[...]], axis=0)
+    def multiply():
         for t in range(count):
-            product[c, t] = lax.dot_general(
-                both,
-                tiles[t, c * width : (c + 1) * width, :],
-                (((1,), (1,)), ((), ())),
-                preferred_element_type=F32,
-            )
+            total = None
+            for w in range(VB):
+                both = jnp.concatenate([wall[w], wall_in[w]], axis=0)
+                cut = slice(w * view, (w + 1) * view)
+                if t < turned.shape[0]:
+                    value = jnp.dot(both, turned[t, cut, :], preferred_element_type=F32)
+                else:
+                    value = lax.dot_general(
+                        both,
+                        tiles[t, :, cut],
+                        (((1,), (1,)), ((), ())),
+                        preferred_element_type=F32,
+                    )
+                total = value if total is None else total + value
+            for c in range(cuts):
+                product[c, t] = total[:, c * width : (c + 1) * width]
 
     def partial(c, s):
         total = None
@@ -485,42 +527,49 @@
         image[half, :, span] = same
         image[1 - half, :, span] = other
 
-    multiply(0)
-    give(0)
-    for c in range(1, cuts):
-        multiply(c)
+    for w in range(VB):
+        wall_copy(w).wait_recv()
+    multiply()
+    for c in range(cuts):
         give(c)
-        pass_on(c - 1)
+    for c in range(cuts - 1):
+        pass_on(c)
     pass_on(cuts - 1)
+
+    totals = []
     for c in range(cuts):
         collect(c)
-
-    spread = [jnp.zeros((rows, sector), F32) for _ in range(2 * HALO + 1)]
-    for p in range(frames // 2):
-        taps = coefs[p * pair : (p + 1) * pair, :].astype(F32)
-        for i in range(2):
-            f = 2 * p + i
-            column = columns[f]
-            g = f % (frames // 2)
-            slices = image[f // (frames // 2), g * rows : (g + 1) * rows, :]
-            for k in range(TAPS):
-                start = (i * TAPS + k) * rows
-                term = taps[start : start + rows] * slices
-                for j in range(HALO + 1):
-                    spread[k + j] = spread[k + j] + jnp.where(
-                        column == float(j - HALO), term, 0.0
-                    )
-    total = None
-    for m in range(2 * HALO + 1):
-        pieces = [jnp.zeros((m, sector), F32)] if m else []
-        pieces.append(spread[m])
-        if m < 2 * HALO:
-            pieces.append(jnp.zeros((2 * HALO - m, sector), F32))
-        padded = jnp.concatenate(pieces, axis=0)
-        total = padded if total is None else total + padded
-    adj_out[0] = total[:HALO]
-    adj_out[1] = total[rows + HALO :]
-    exchange(adj_out, adj_in, ha_send, ha_recv)
+        span = slice(c * width, (c + 1) * width)
+        spread = [jnp.zeros((rows, width), F32) for _ in range(2 * HALO + 1)]
+        for p in range(frames // 2):
+            taps = coefs[p * pair : (p + 1) * pair, span].astype(F32)
+            for i in range(2):
+                f = 2 * p + i
+                column = columns[f]
+                g = f % (frames // 2)
+                slices = image[f // (frames // 2), g * rows : (g + 1) * rows, span]
+                for k in range(TAPS):
+                    start = (i * TAPS + k) * rows
+                    term = taps[start : start + rows] * slices
+                    for j in range(HALO + 1):
+                        spread[k + j] = spread[k + j] + jnp.where(
+                            column == float(j - HALO), term, 0.0
+                        )
+        total = None
+        for m in range(2 * HALO + 1):
+            pieces = [jnp.zeros((m, width), F32)] if m else []
+            pieces.append(spread[m])
+            if m < 2 * HALO:
+                pieces.append(jnp.zeros((2 * HALO - m, width), F32))
+            padded = jnp.concatenate(pieces, axis=0)
+            total = padded if total is None else total + padded
+        adj_out[0, :, span] = total[:HALO]
+        adj_out[1, :, span] = total[rows + HALO :]
+        totals.append(total[HALO : rows + HALO])
+    exchange(adj_out, edges_hbm, ha_send, ha_recv)
+    base[...] = vol + voxel_weight[...] * jnp.concatenate(totals, axis=1)
+    out_base = pltpu.make_async_copy(base, base_hbm, out_sem.at[0])
+    out_base.start()
     for j in range(2):
         for dh, dp in others:
             cross(dh, dp, j).wait_send()
@@ -528,28 +577,62 @@
             to_sibling(dh, dp, j).wait_send()
     for copy in partner_copies:
         copy.wait_send()
-    for n in range(parts):
-        proj_copy(n).wait_send()
-    wall_copy.wait_send()
-    back_copy.wait()
-    out_weighted.wait()
+    for w in range(VB):
+        proj_copy(w).wait_send()
+        wall_copy(w).wait_send()
+        back_copy(w).wait()
+        out_weighted(w).wait()
     for c in range(cuts):
         sib_copy(c).wait_send()
         for dh, dp in others:
             far_copy(c, dh, dp).wait_send()
-    exchange_wait(adj_out, adj_in, ha_send, ha_recv)
-    middle = jnp.zeros((rows - 2 * HALO, sector), F32)
-    edges = jnp.concatenate([adj_in[0], middle, adj_in[1]], axis=0)
-    adjoint = total[HALO : rows + HALO] + edges
-    next_ref[...] = vol + voxel_weight[...] * adjoint
-    out_next = pltpu.make_async_copy(next_ref, next_hbm, out_sem.at[1])
+
+    @pl.when(slab == 0)
+    def _():
+        pltpu.make_async_copy(zeros, edges_hbm.at[0], zero_sem.at[0]).wait()
+
+    @pl.when(slab == slabs - 1)
+    def _():
+        pltpu.make_async_copy(zeros, edges_hbm.at[1], zero_sem.at[0]).wait()
+
+    out_base.wait()
+    exchange_wait(adj_out, edges_hbm, ha_send, ha_recv)
+
+
+def settle(
+    base_in,
+    edges_in,
+    scale_in,
+    weighted_in,
+    next_out,
+    weighted_out,
+    base,
+    edges,
+    scale,
+    rows,
+    in_sem,
+    out_sem,
+):
+    loads = [
+        pltpu.make_async_copy(src, dst, in_sem.at[n])
+        for n, (src, dst) in enumerate(
+            ((weighted_in, rows), (base_in, base), (edges_in, edges), (scale_in, scale))
+        )
+    ]
+    for load in loads:
+        load.start()
+    out_rows = pltpu.make_async_copy(rows, weighted_out, out_sem.at[0])
+    out_next = pltpu.make_async_copy(base, next_out, out_sem.at[1])
+    loads[0].wait()
+    out_rows.start()
+    for load in loads[1:]:
+        load.wait()
+    middle = jnp.zeros((base.shape[0] - 2 * HALO, base.shape[1]), F32)
+    adjoint = jnp.concatenate([edges[0], middle, edges[1]], axis=0)
+    base[...] = base[...] + scale[...] * adjoint
     out_next.start()
+    out_rows.wait()
     out_next.wait()
-
-
-def settle(next_in, weighted_in, next_out, weighted_out):
-    next_out[...] = next_in[...]
-    weighted_out[...] = weighted_in[...]
 
 
 def body(
@@ -571,20 +654,20 @@
     stacked = frames * rows
     chips = blocks // 2
     mine = tiles.shape[0] // 2
-    parts = rays // 256
+    view = rays // VB
     cuts = 2
-    vmem = pl.BlockSpec(memory_space=pltpu.VMEM)
     hbm = pl.BlockSpec(memory_space=pl.ANY)
     dma = pltpu.SemaphoreType.DMA
     flops = 4 * stacked * blocks * sector * rays
-    volume_next, weighted = pl.pallas_call(
+    base, edges, weighted = pl.pallas_call(
         functools.partial(kernel, blocks, slabs, frames, rows),
         out_shape=(
             jax.ShapeDtypeStruct(volume.shape, F32),
+            jax.ShapeDtypeStruct((2, HALO, sector), F32),
             jax.ShapeDtypeStruct((stacked, rays), BF16),
         ),
         in_specs=[hbm] * 10,
-        out_specs=(hbm, hbm),
+        out_specs=(hbm, hbm, hbm),
         scratch_shapes=[
             pltpu.VMEM(volume.shape, F32),
             pltpu.VMEM((stacked // 2, rays), BF16),
@@ -597,20 +680,21 @@
             pltpu.SMEM(conj_view.shape, jnp.int32),
             pltpu.SMEM((4, mine), jnp.int32),
             pltpu.VMEM(volume.shape, F32),
+            pltpu.VMEM((HALO, sector), F32),
             pltpu.VMEM((mine,) + tiles.shape[1:], BF16),
+            pltpu.VMEM((3, rays, sector), BF16),
             pltpu.VMEM((blocks, 2, stacked // 4, sector), BF16),
             pltpu.VMEM((2, stacked // 4, sector), BF16),
-            pltpu.VMEM((parts, stacked, 256), F32),
-            pltpu.VMEM((parts, stacked, 256), F32),
-            pltpu.VMEM((parts, stacked, 256), F32),
+            pltpu.VMEM((VB, stacked, view), F32),
+            pltpu.VMEM((VB, stacked, view), F32),
+            pltpu.VMEM((VB, stacked, view), F32),
             pltpu.VMEM((stacked // 2, rays), BF16),
             pltpu.VMEM(ray_weight.shape, F32),
             pltpu.VMEM((rays,), F32),
-            pltpu.VMEM((stacked, rays), BF16),
-            pltpu.VMEM((stacked, rays), BF16),
+            pltpu.VMEM((VB, stacked, view), BF16),
+            pltpu.VMEM((VB, stacked, view), BF16),
             pltpu.VMEM((cuts, mine, 2 * stacked, sector // cuts), F32),
             pltpu.VMEM((2, stacked // 2, sector), F32),
-            pltpu.VMEM((2, HALO, sector), F32),
             pltpu.VMEM((2, HALO, sector), F32),
             pltpu.VMEM((2, HALO, sector), F32),
             pltpu.VMEM((2, HALO, sector), F32),
@@ -619,7 +703,8 @@
             pltpu.VMEM((cuts, chips, stacked // 2, sector // cuts), BF16),
             pltpu.VMEM((cuts, chips, stacked // 2, sector // cuts), BF16),
             dma((9,)),
-            dma((2,)),
+            dma((1 + VB,)),
+            dma((1,)),
             dma((mine,)),
             dma((chips, 2)),
             dma((chips, 2)),
@@ -627,10 +712,10 @@
             dma((chips, 2)),
             dma((3,)),
             dma((3,)),
-            dma((parts,)),
-            dma((parts,)),
-            dma((2,)),
-            dma((2,)),
+            dma((VB,)),
+            dma((VB,)),
+            dma((2, VB)),
+            dma((2, VB)),
             dma((2,)),
             dma((2,)),
             dma((2,)),
@@ -664,9 +749,17 @@
             jax.ShapeDtypeStruct(volume.shape, F32),
             jax.ShapeDtypeStruct((stacked, rays), BF16),
         ),
-        in_specs=[vmem, vmem],
-        out_specs=(vmem, vmem),
-    )(volume_next, weighted)
+        in_specs=[hbm] * 4,
+        out_specs=(hbm, hbm),
+        scratch_shapes=[
+            pltpu.VMEM(volume.shape, F32),
+            pltpu.VMEM((2, HALO, sector), F32),
+            pltpu.VMEM(volume.shape, F32),
+            pltpu.VMEM((stacked, rays), BF16),
+            dma((4,)),
+            dma((2,)),
+        ],
+    )(base, edges, voxel_weight, weighted)
     return volume_next, weighted.reshape(frames, rows, rays)
 
 

time: 35.1 us -> 32 us (0.912)
  Pallas kernels: 34.3 us -> 31.2 us
    pallas_call x1, Pallas kernels: 32.7 us -> 29.5 us  [body(): pl.pallas_call(functools.partial(kernel, blocks, slabs, frames, rows), ou...]
where the time goes in v2:
time: 32 us; the launch traced here: 31.8 us
  Pallas kernels  31.2 us (98%)
  between operations  0.64 us (2%)
    pallas_call x1, Pallas kernels, body(): pl.pallas_call(functools.partial(kernel, blocks, slabs, frames, rows), ou...  29.5 us
    pallas_call x1, Pallas kernels, body(): pl.pallas_call(settle, out_shape=(jax.ShapeDtypeStruct(volume.shape, F32)...  1.66 us

profile of v2, /device:TPU:0, one launch (start us, length us, event | category | flops | bytes accessed | tf_op | source)
XLA Modules:
  0.0 31.8 jit_solution(8614217953589597005)
XLA Ops:
  0.6 29.5 %shard_map.113 = (f32[8,1024]{1,0:T(8,128)}, f32[2,2,1024]{2,1,0:T(2,128)}, bf16[64,1536]{1,0:T(8,128)(2,1)}) custom-call(f32[8,1024]{1,0:T(8,128)} %volume_hbm.1, bf16[64,1536]{1,0:T(8,128)(2,1)} %bitcast.4, bf16[8,1024,1536]{2,1,0:T(8,128)(2,1)} %tiles_hbm.1, s32[8,8]{1,0:T(8,128)} %index_hbm.1, bf16[192,1024]{1,0:T(8,128)(2,1)} %bitcast.3, ...), custom_call_target="tpu_custom_call" | custom-call | flops 3221225472 | bytes 25165824 | tf_op jit(solution)/shard_map/pallas_call | solution.py:662
  30.2 1.7 %shard_map.114 = (f32[8,1024]{1,0:T(8,128)}, bf16[64,1536]{1,0:T(8,128)(2,1)}) custom-call(f32[8,1024]{1,0:T(8,128)} %get-tuple-element.7.base_in, f32[2,2,1024]{2,1,0:T(2,128)} %get-tuple-element.8.edges_in, f32[8,1024]{1,0:T(8,128)} %scale_in.1, bf16[64,1536]{1,0:T(8,128)(2,1)} %get-tuple-element.9.weighted_in), custom_call_target="tpu_custom_call" | custom-call | tf_op jit(solution)/shard_map/pallas_call | solution.py:746

commit v3 on v2

--- a/solution.py
+++ b/solution.py
@@ -43,8 +43,10 @@
     tile_index,
     conj_view,
     find,
+    pick,
     base,
     zeros,
+    omega,
     tiles,
     turned,
     gathered,
@@ -134,9 +136,10 @@
     barrier = pltpu.get_barrier_semaphore()
     pl.semaphore_signal(barrier, inc=1, device_id=(sibling, slab), device_id_type=MESH)
     for dh, dp in others:
-        pl.semaphore_signal(
-            barrier, inc=1, device_id=(2 * chip_at(dh, dp) + core, slab), device_id_type=MESH
-        )
+        for other in (core, 1 - core):
+            pl.semaphore_signal(
+                barrier, inc=1, device_id=(2 * chip_at(dh, dp) + other, slab), device_id_type=MESH
+            )
 
     @pl.when(has_low)
     def _():
@@ -173,7 +176,7 @@
     vol_out[0] = vol[:HALO]
     vol_out[1] = vol[rows - HALO :]
 
-    peers = chips + has_low.astype(jnp.int32) + has_high.astype(jnp.int32)
+    peers = blocks - 1 + has_low.astype(jnp.int32) + has_high.astype(jnp.int32)
     pl.semaphore_wait(barrier, peers)
 
     def halo(out, into, send, recv, side):
@@ -251,8 +254,8 @@
         return remote(
             away.at[j] if dh else gathered.at[me, j],
             gathered.at[me, j],
-            ag_send.at[slot(dh, dp), j],
-            ag_recv.at[slot(dh, dp), j],
+            ag_send.at[slot(dh, dp) - 1, j],
+            ag_recv.at[slot(dh, dp) - 1, j],
             2 * chip_at(dh, dp) + core,
         )
 
@@ -329,6 +332,13 @@
             for s in range(blocks):
                 at = jnp.where(row[s] == first + t, s, at)
             find[q, t] = at
+    for i, (dh, dp) in enumerate(everyone):
+        for n in range(2):
+            s = 2 * chip_at(dh, dp) + (core if bool(n) == (i == 0) else 1 - core)
+            for q in range(4):
+                t = tile_index[group[q], s] - first
+                ours = jnp.logical_and(t >= 0, t < count)
+                pick[2 * i + n, q] = jnp.where(ours, t, count)
 
     pass_chunk(0)
     turn(2)
@@ -357,6 +367,7 @@
 
     for w in range(VB):
         proj_copy(w).start()
+    product[:, count] = jnp.zeros_like(product[:, count])
     for copy in local[4:]:
         copy.wait()
     for copy in partner_copies:
@@ -450,6 +461,19 @@
         back_copy(w).start()
         out_weighted(w).start()
 
+    for p in range(frames // 2):
+        taps = coefs[p * pair : (p + 1) * pair, :].astype(F32)
+        for i in range(2):
+            f = 2 * p + i
+            masks = [columns[f] == float(j - HALO) for j in range(HALO + 1)]
+            for m in range(2 * HALO + 1):
+                value = None
+                for k in range(max(0, m - HALO), min(TAPS, m + 1)):
+                    start = (i * TAPS + k) * rows
+                    term = jnp.where(masks[m - k], taps[start : start + rows], 0.0)
+                    value = term if value is None else value + term
+                omega[f, m] = value
+
     cuts = product.shape[0]
     width = sector // cuts
 
@@ -472,13 +496,10 @@
             for c in range(cuts):
                 product[c, t] = total[:, c * width : (c + 1) * width]
 
-    def partial(c, s):
+    def partial(c, i, n):
         total = None
         for q in range(4):
-            t = tile_index[group[q], s] - first
-            ours = jnp.logical_and(t >= 0, t < count)
-            t = jnp.where(ours, t, 0)
-            term = jnp.where(ours, product[c, t, q * stacked : (q + 1) * stacked, :], 0.0)
+            term = product[c, pick[2 * i + n, q], q * stacked : (q + 1) * stacked, :]
             total = term if total is None else total + term
         return total
 
@@ -490,20 +511,20 @@
         return remote(
             far_out.at[c, i],
             far_in.at[c, i],
-            fr_send.at[c, i],
-            fr_recv.at[c, i],
-            2 * chip_at(dh, dp) + core,
+            fr_send.at[c, i - 1],
+            fr_recv.at[c, i - 1],
+            2 * chip_at(dh, dp) + 1 - core,
         )
 
     def give(c):
-        for dh, dp in everyone:
-            sib_out[c, slot(dh, dp)] = partial(c, 2 * chip_at(dh, dp) + 1 - core).astype(BF16)
+        for i, (dh, dp) in enumerate(everyone):
+            sib_out[c, slot(dh, dp)] = partial(c, i, 0).astype(BF16)
         sib_copy(c).start()
 
     def pass_on(c):
         for n, (dh, dp) in enumerate(reversed(everyone)):
             i = slot(dh, dp)
-            value = partial(c, 2 * chip_at(dh, dp) + core)
+            value = partial(c, everyone.index((dh, dp)), 1)
             if n == 0:
                 sib_copy(c).wait_recv()
             value = value + sib_in[c, i].astype(F32)
@@ -540,21 +561,13 @@
     for c in range(cuts):
         collect(c)
         span = slice(c * width, (c + 1) * width)
-        spread = [jnp.zeros((rows, width), F32) for _ in range(2 * HALO + 1)]
-        for p in range(frames // 2):
-            taps = coefs[p * pair : (p + 1) * pair, span].astype(F32)
-            for i in range(2):
-                f = 2 * p + i
-                column = columns[f]
-                g = f % (frames // 2)
-                slices = image[f // (frames // 2), g * rows : (g + 1) * rows, span]
-                for k in range(TAPS):
-                    start = (i * TAPS + k) * rows
-                    term = taps[start : start + rows] * slices
-                    for j in range(HALO + 1):
-                        spread[k + j] = spread[k + j] + jnp.where(
-                            column == float(j - HALO), term, 0.0
-                        )
+        spread = [None] * (2 * HALO + 1)
+        for f in range(frames):
+            g = f % (frames // 2)
+            slices = image[f // (frames // 2), g * rows : (g + 1) * rows, span]
+            for m in range(2 * HALO + 1):
+                term = omega[f, m, :, span] * slices
+                spread[m] = term if spread[m] is None else spread[m] + term
         total = None
         for m in range(2 * HALO + 1):
             pieces = [jnp.zeros((m, width), F32)] if m else []
@@ -679,8 +692,10 @@
             pltpu.SMEM(tile_index.shape, jnp.int32),
             pltpu.SMEM(conj_view.shape, jnp.int32),
             pltpu.SMEM((4, mine), jnp.int32),
+            pltpu.SMEM((2 * chips, 4), jnp.int32),
             pltpu.VMEM(volume.shape, F32),
             pltpu.VMEM((HALO, sector), F32),
+            pltpu.VMEM((frames, 2 * HALO + 1, rows, sector), F32),
             pltpu.VMEM((mine,) + tiles.shape[1:], BF16),
             pltpu.VMEM((3, rays, sector), BF16),
             pltpu.VMEM((blocks, 2, stacked // 4, sector), BF16),
@@ -693,7 +708,7 @@
             pltpu.VMEM((rays,), F32),
             pltpu.VMEM((VB, stacked, view), BF16),
             pltpu.VMEM((VB, stacked, view), BF16),
-            pltpu.VMEM((cuts, mine, 2 * stacked, sector // cuts), F32),
+            pltpu.VMEM((cuts, mine + 1, 2 * stacked, sector // cuts), F32),
             pltpu.VMEM((2, stacked // 2, sector), F32),
             pltpu.VMEM((2, HALO, sector), F32),
             pltpu.VMEM((2, HALO, sector), F32),
@@ -706,8 +721,8 @@
             dma((1 + VB,)),
             dma((1,)),
             dma((mine,)),
-            dma((chips, 2)),
-            dma((chips, 2)),
+            dma((chips - 1, 2)),
+            dma((chips - 1, 2)),
             dma((chips, 2)),
             dma((chips, 2)),
             dma((3,)),
@@ -722,8 +737,8 @@
             dma((2,)),
             dma((cuts,)),
             dma((cuts,)),
-            dma((cuts, chips)),
-            dma((cuts, chips)),
+            dma((cuts, chips - 1)),
+            dma((cuts, chips - 1)),
         ],
         cost_estimate=pl.CostEstimate(
             flops=flops, bytes_accessed=2 * tiles.size, transcendentals=0

time: 32 us -> 30.5 us (0.953)
  Pallas kernels: 31.2 us -> 29.7 us
    pallas_call x1, Pallas kernels: 29.5 us -> 28.1 us  [body(): pl.pallas_call(functools.partial(kernel, blocks, slabs, frames, rows), ou...]
where the time goes in v3:
time: 30.5 us; the launch traced here: 30.4 us
  Pallas kernels  29.7 us (97%)
  between operations  0.64 us (2%)
    pallas_call x1, Pallas kernels, body(): pl.pallas_call(functools.partial(kernel, blocks, slabs, frames, rows), ou...  28.1 us
    pallas_call x1, Pallas kernels, body(): pl.pallas_call(settle, out_shape=(jax.ShapeDtypeStruct(volume.shape, F32)...  1.66 us

profile of v3, /device:TPU:0, one launch (start us, length us, event | category | flops | bytes accessed | tf_op | source)
XLA Modules:
  0.0 30.4 jit_solution(15397915522119819060)
XLA Ops:
  0.6 28.1 %shard_map.113 = (f32[8,1024]{1,0:T(8,128)}, f32[2,2,1024]{2,1,0:T(2,128)}, bf16[64,1536]{1,0:T(8,128)(2,1)}) custom-call(f32[8,1024]{1,0:T(8,128)} %volume_hbm.1, bf16[64,1536]{1,0:T(8,128)(2,1)} %bitcast.4, bf16[8,1024,1536]{2,1,0:T(8,128)(2,1)} %tiles_hbm.1, s32[8,8]{1,0:T(8,128)} %index_hbm.1, bf16[192,1024]{1,0:T(8,128)(2,1)} %bitcast.3, ...), custom_call_target="tpu_custom_call" | custom-call | flops 3221225472 | bytes 25165824 | tf_op jit(solution)/shard_map/pallas_call | solution.py:675
  28.7 1.7 %shard_map.114 = (f32[8,1024]{1,0:T(8,128)}, bf16[64,1536]{1,0:T(8,128)(2,1)}) custom-call(f32[8,1024]{1,0:T(8,128)} %get-tuple-element.7.base_in, f32[2,2,1024]{2,1,0:T(2,128)} %get-tuple-element.8.edges_in, f32[8,1024]{1,0:T(8,128)} %scale_in.1, bf16[64,1536]{1,0:T(8,128)(2,1)} %get-tuple-element.9.weighted_in), custom_call_target="tpu_custom_call" | custom-call | tf_op jit(solution)/shard_map/pallas_call | solution.py:761

commit v4 on v3

--- a/solution.py
+++ b/solution.py
@@ -626,25 +626,34 @@
     in_sem,
     out_sem,
 ):
+    pieces = 4
+    each = rows.shape[0] // pieces
+    spans = [pl.ds(n * each, each) for n in range(pieces)]
     loads = [
         pltpu.make_async_copy(src, dst, in_sem.at[n])
         for n, (src, dst) in enumerate(
-            ((weighted_in, rows), (base_in, base), (edges_in, edges), (scale_in, scale))
+            [(base_in, base), (edges_in, edges), (scale_in, scale)]
+            + [(weighted_in.at[span], rows.at[span]) for span in spans]
         )
     ]
     for load in loads:
         load.start()
-    out_rows = pltpu.make_async_copy(rows, weighted_out, out_sem.at[0])
-    out_next = pltpu.make_async_copy(base, next_out, out_sem.at[1])
-    loads[0].wait()
-    out_rows.start()
-    for load in loads[1:]:
+    stores = [
+        pltpu.make_async_copy(rows.at[span], weighted_out.at[span], out_sem.at[n])
+        for n, span in enumerate(spans)
+    ]
+    out_next = pltpu.make_async_copy(base, next_out, out_sem.at[pieces])
+    for load in loads[:3]:
         load.wait()
     middle = jnp.zeros((base.shape[0] - 2 * HALO, base.shape[1]), F32)
     adjoint = jnp.concatenate([edges[0], middle, edges[1]], axis=0)
     base[...] = base[...] + scale[...] * adjoint
     out_next.start()
-    out_rows.wait()
+    for load, store in zip(loads[3:], stores):
+        load.wait()
+        store.start()
+    for store in stores:
+        store.wait()
     out_next.wait()
 
 
@@ -771,8 +780,8 @@
             pltpu.VMEM((2, HALO, sector), F32),
             pltpu.VMEM(volume.shape, F32),
             pltpu.VMEM((stacked, rays), BF16),
-            dma((4,)),
-            dma((2,)),
+            dma((7,)),
+            dma((5,)),
         ],
     )(base, edges, voxel_weight, weighted)
     return volume_next, weighted.reshape(frames, rows, rays)

time: 30.5 us -> 30.5 us (level)
  no operation moved by 1% of the time
where the time goes in v4:
time: 30.5 us; the launch traced here: 30.4 us
  Pallas kernels  29.7 us (97%)
  between operations  0.64 us (2%)
    pallas_call x1, Pallas kernels, body(): pl.pallas_call(functools.partial(kernel, blocks, slabs, frames, rows), ou...  28.1 us
    pallas_call x1, Pallas kernels, body(): pl.pallas_call(settle, out_shape=(jax.ShapeDtypeStruct(volume.shape, F32)...  1.65 us

profile of v4, /device:TPU:0, one launch (start us, length us, event | category | flops | bytes accessed | tf_op | source)
XLA Modules:
  0.0 30.4 jit_solution(5581915029954688140)
XLA Ops:
  0.6 28.1 %shard_map.113 = (f32[8,1024]{1,0:T(8,128)}, f32[2,2,1024]{2,1,0:T(2,128)}, bf16[64,1536]{1,0:T(8,128)(2,1)}) custom-call(f32[8,1024]{1,0:T(8,128)} %volume_hbm.1, bf16[64,1536]{1,0:T(8,128)(2,1)} %bitcast.4, bf16[8,1024,1536]{2,1,0:T(8,128)(2,1)} %tiles_hbm.1, s32[8,8]{1,0:T(8,128)} %index_hbm.1, bf16[192,1024]{1,0:T(8,128)(2,1)} %bitcast.3, ...), custom_call_target="tpu_custom_call" | custom-call | flops 3221225472 | bytes 25165824 | tf_op jit(solution)/shard_map/pallas_call | solution.py:684
  28.7 1.7 %shard_map.114 = (f32[8,1024]{1,0:T(8,128)}, bf16[64,1536]{1,0:T(8,128)(2,1)}) custom-call(f32[8,1024]{1,0:T(8,128)} %get-tuple-element.7.base_in, f32[2,2,1024]{2,1,0:T(2,128)} %get-tuple-element.8.edges_in, f32[8,1024]{1,0:T(8,128)} %scale_in.1, bf16[64,1536]{1,0:T(8,128)(2,1)} %get-tuple-element.9.weighted_in), custom_call_target="tpu_custom_call" | custom-call | tf_op jit(solution)/shard_map/pallas_call | solution.py:770
